TPU v7x, 512 devices: a whole 4x4x16 slice. The times are simulated.
512 devices in a mesh: section: 8 (over x, core), expert: 8 (over z_lo), dp: 8 (over y, z_hi).
Axes of the slice: x: 4, y: 4, z: 16 (z_hi: 2, z_lo: 8; z = z_hi * 8 + z_lo), core: 2. Of those that a mesh axis runs over, the one named last changes fastest.
Arguments:
- layer_input: bfloat16 [8, 8192, 2048], P('section', ('expert', 'dp')), may hold values from -6 to 6
- output_grad: bfloat16 [8, 8192, 2048], P('section', ('expert', 'dp')), may hold values from -6 to 6
- expert_ids: int32 [8, 8192], P('section', ('expert', 'dp')), may hold values from 0 to 63, as said below
- w_gate: bfloat16 [8, 2048, 8192], P('section', None, ('expert', 'dp')), may hold values from -0.125 to 0.125
- w_up: bfloat16 [8, 2048, 8192], P('section', None, ('expert', 'dp')), may hold values from -0.125 to 0.125
- w_down: bfloat16 [8, 2048, 8192], P('section', None, ('expert', 'dp')), may hold values from -0.0625 to 0.0625
Outputs:
- input_grad: bfloat16 [8, 8192, 2048], P('section', ('expert', 'dp'))
- grad_gate: bfloat16 [8, 2048, 8192], P('section', None, ('expert', 'dp'))
- grad_up: bfloat16 [8, 2048, 8192], P('section', None, ('expert', 'dp'))
- grad_down: bfloat16 [8, 2048, 8192], P('section', None, ('expert', 'dp'))
Inputs may be any that keep to these rules, and one draw needn't show every extreme that they name: `expert_ids`: expert 0 is the expert of these weights. Every device's 128 tokens name expert 0 between 1 and 8 times, and on every section some device names it exactly 8 times.
All inputs are finite; a program needn't handle non-finite values.
Results may differ from a plain program's by a relative error of at most 0.0065.
Values may be sent and summed in bfloat16 or wider, within the bound.
A program may use at most 64 MiB of HBM per device.

v0:
```python
import jax
import jax.numpy as jnp
from jax import lax
from jax.sharding import PartitionSpec as P

SLOT = 8


def shifted(value, axis, steps):
    count = lax.axis_size(axis)
    pairs = [(source, (source + steps) % count) for source in range(count)]
    return lax.ppermute(value, axis, pairs)


def unit_grads(x_rows, dy_rows, w_gate, w_up, w_down):
    gate = jnp.dot(x_rows, w_gate, preferred_element_type=jnp.float32)
    upper = jnp.dot(x_rows, w_up, preferred_element_type=jnp.float32)
    sigma = jax.nn.sigmoid(gate)
    active = gate * sigma
    hidden = (active * upper).astype(jnp.bfloat16)
    d_hidden = jnp.dot(dy_rows, w_down, preferred_element_type=jnp.float32)
    d_gate = (d_hidden * upper * sigma * (1.0 + gate * (1.0 - sigma))).astype(jnp.bfloat16)
    d_up = (d_hidden * active).astype(jnp.bfloat16)
    back_dims = (((1,), (1,)), ((), ()))
    d_input = lax.dot_general(d_gate, w_gate, back_dims, preferred_element_type=jnp.float32)
    d_input = d_input + lax.dot_general(d_up, w_up, back_dims, preferred_element_type=jnp.float32)
    return (d_input, d_gate, d_up, hidden)


def weight_grads(x_rows, dy_rows, d_gate, d_up, hidden):
    row_dims = (((0,), (0,)), ((), ()))
    part_gate = lax.dot_general(x_rows, d_gate, row_dims, preferred_element_type=jnp.float32)
    part_up = lax.dot_general(x_rows, d_up, row_dims, preferred_element_type=jnp.float32)
    part_down = lax.dot_general(dy_rows, hidden, row_dims, preferred_element_type=jnp.float32)
    return (part_gate, part_up, part_down)


def body(layer_input, output_grad, expert_ids, w_gate, w_up, w_down):
    inputs = layer_input[0]
    grads = output_grad[0]
    routes = expert_ids[0]
    chosen = (routes == 0).astype(jnp.int32)
    order = jnp.arange(chosen.shape[0], dtype=jnp.int32)
    within = jnp.sum(jnp.where(order[None, :] < order[:, None], chosen[None, :], 0), axis=1)
    target = jnp.where(chosen > 0, within, SLOT)
    places = jnp.arange(SLOT, dtype=jnp.int32)
    match = (target[None, :] == places[:, None]).astype(jnp.bfloat16)
    send_x = jnp.dot(match, inputs, preferred_element_type=jnp.float32).astype(jnp.bfloat16)
    send_dy = jnp.dot(match, grads, preferred_element_type=jnp.float32).astype(jnp.bfloat16)
    group_x, group_dy = (
        lax.all_gather(send_x, "expert", axis=0, tiled=True),
        lax.all_gather(send_dy, "expert", axis=0, tiled=True),
    )
    full_gate, full_up, full_down = (
        lax.all_gather(w_gate[0], "dp", axis=1, tiled=True),
        lax.all_gather(w_up[0], "dp", axis=1, tiled=True),
        lax.all_gather(w_down[0], "dp", axis=1, tiled=True),
    )
    d_part, d_gate, d_up, hidden = unit_grads(group_x, group_dy, full_gate, full_up, full_down)
    mine = lax.psum_scatter(d_part.astype(jnp.bfloat16), "expert", scatter_dimension=0, tiled=True)
    own_gate, own_up, own_hidden = (
        lax.all_to_all(d_gate, "dp", split_axis=1, concat_axis=0, tiled=True),
        lax.all_to_all(d_up, "dp", split_axis=1, concat_axis=0, tiled=True),
        lax.all_to_all(hidden, "dp", split_axis=1, concat_axis=0, tiled=True),
    )
    every_x, every_dy = (
        lax.all_gather(group_x, "dp", axis=0, tiled=True),
        lax.all_gather(group_dy, "dp", axis=0, tiled=True),
    )
    part_gate, part_up, part_down = weight_grads(every_x, every_dy, own_gate, own_up, own_hidden)
    d_rows = lax.optimization_barrier(mine)
    term = lax.dot_general(
        match, d_rows, (((0,), (0,)), ((), ())), preferred_element_type=jnp.float32
    )
    token_grad = (grads.astype(jnp.float32) + term).astype(jnp.bfloat16)
    moved = shifted(token_grad, "section", -1)
    return (
        moved[None],
        part_gate.astype(jnp.bfloat16)[None],
        part_up.astype(jnp.bfloat16)[None],
        part_down.astype(jnp.bfloat16)[None],
    )


def solution(mesh):
    in_specs = (
        P("section", ("expert", "dp"), None),
        P("section", ("expert", "dp"), None),
        P("section", ("expert", "dp")),
        P("section", None, ("expert", "dp")),
        P("section", None, ("expert", "dp")),
        P("section", None, ("expert", "dp")),
    )
    out_specs = (
        P("section", ("expert", "dp"), None),
        P("section", None, ("expert", "dp")),
        P("section", None, ("expert", "dp")),
        P("section", None, ("expert", "dp")),
    )
    return jax.shard_map(body, mesh=mesh, in_specs=in_specs, out_specs=out_specs, check_vma=False)
```

profile of v0, /device:TPU:16, one launch (start us, length us, event | category | flops | bytes accessed | tf_op | source)
XLA Modules:
  0.0 865.1 jit_solution(10704545008492486408)
XLA Ops:
  7.2 0.7 all-gather.17.cloned.1.call-update
  8.0 0.7 all-gather.15.cloned.1.call-update
  8.7 0.7 all-gather.13.cloned.1.call-update
  9.4 0.7 fusion.28
  10.2 0.7 fusion.27
  11.1 57.3 %all_gather.23 = bf16[64,2048]{1,0:T(8,128)(2,1)S(1)} all-gather(bf16[8,2048]{1,0:T(8,128)(2,1)S(1)} %convolution_convert_fusion.3), channel_id=1, replica_groups=mesh['section'=8,'expert'=8,'dp'=8] {'expert'}, dimensions={0}, use_global_device_ids=true | all-gather | bytes 294912 | tf_op jit(solution)/shard_map/all_gather | solution.py:51
  68.4 1.3 convolution_convert_fusion.4
  69.7 84.0 %all_gather.21 = bf16[64,2048]{1,0:T(8,128)(2,1)S(1)} all-gather(bf16[8,2048]{1,0:T(8,128)(2,1)S(1)} %convolution_convert_fusion.4), channel_id=1, replica_groups=mesh['section'=8,'expert'=8,'dp'=8] {'expert'}, dimensions={0}, use_global_device_ids=true | all-gather | bytes 294912 | tf_op jit(solution)/shard_map/all_gather | solution.py:52
  153.8 48.7 %all-gather.17.cloned.1.call-done = bf16[1,2048,1024]{2,1,0:T(8,128)(2,1)} async-done(((bf16[1,2048,128]{2,1,0:T(8,128)(2,1)}), bf16[1,2048,1024]{2,1,0:T(8,128)(2,1)}) %all-gather.17.cloned.1.call-update) | async-done | bytes 4194320 | tf_op jit(solution)/shard_map/all_gather | solution.py:55
  202.5 3.0 fusion.2
  205.5 174.7 %all-gather.15.cloned.1.call-done = bf16[1,2048,1024]{2,1,0:T(8,128)(2,1)} async-done(((bf16[1,2048,128]{2,1,0:T(8,128)(2,1)}), bf16[1,2048,1024]{2,1,0:T(8,128)(2,1)}) %all-gather.15.cloned.1.call-update) | async-done | bytes 4194320 | tf_op jit(solution)/shard_map/all_gather | solution.py:56
  380.2 3.0 fusion.6
  383.2 175.2 %all-gather.13.cloned.1.call-done = bf16[1,2048,1024]{2,1,0:T(8,128)(2,1)} async-done(((bf16[1,2048,128]{2,1,0:T(8,128)(2,1)}), bf16[1,2048,1024]{2,1,0:T(8,128)(2,1)}) %all-gather.13.cloned.1.call-update) | async-done | bytes 4194320 | tf_op jit(solution)/shard_map/all_gather | solution.py:57
  558.4 3.2 fusion.23
  561.8 1.4 fusion
  563.2 2.1 fusion.17
  565.4 0.5 all-gather.9.cloned.1.call-update
  566.5 0.7 copy_bitcast_fusion.2
  567.2 5.7 all-to-all-start
  572.9 0.7 copy_bitcast_fusion.1
  573.6 12.6 %all-to-all-done = bf16[64,8,128]{2,0,1:T(8,128)(2,1)S(1)} async-done(((bf16[64,8,128]{2,0,1:T(8,128)(2,1)}), bf16[64,8,128]{2,0,1:T(8,128)(2,1)S(1)}, u32[]{:S(2)}, u32[]{:S(2)}) %all-to-all-start) | async-done | bytes 131104 | tf_op jit(solution)/shard_map/all_to_all | solution.py:62
  586.3 5.8 all-to-all-start.1
  592.0 0.7 copy.22
  592.7 30.8 %reduce-scatter.2.cloned.1.call-done = bf16[8,2048]{1,0:T(8,128)(2,1)} async-done(((bf16[64,2048]{1,0:T(8,128)(2,1)}), bf16[8,2048]{1,0:T(8,128)(2,1)}) %reduce-scatter.2.cloned.1.call-update) | async-done | bytes 32784 | tf_op jit(solution)/shard_map/reduce_scatter | solution.py:60
  623.5 6.7 all-to-all-start.2
  630.2 1.1 fusion.10
  631.3 107.6 %all-gather.9.cloned.1.call-done = bf16[512,2048]{1,0:T(8,128)(2,1)} async-done(((bf16[64,2048]{1,0:T(8,128)(2,1)}), bf16[512,2048]{1,0:T(8,128)(2,1)}) %all-gather.9.cloned.1.call-update) | async-done | bytes 2097168 | tf_op jit(solution)/shard_map/all_gather | solution.py:67
  738.9 3.3 fusion.14
  742.2 1.6 fusion.15
  743.8 110.6 %all-gather.11.cloned.1.call-done = bf16[512,2048]{1,0:T(8,128)(2,1)} async-done(((bf16[64,2048]{1,0:T(8,128)(2,1)}), bf16[512,2048]{1,0:T(8,128)(2,1)}) %all-gather.11.cloned.1.call-update) | async-done | bytes 2097168 | tf_op jit(solution)/shard_map/all_gather | solution.py:68
  854.4 3.1 fusion.16
  857.5 0.8 copy.24
  (28 shorter events, 1.3 us)
Async XLA Ops:
  7.2 3.7 copy-start
  7.2 195.3 %all-gather.17.cloned.1.call-start = ((), (), s32[]{:S(2)}) async-start(), calls=%async_computation.9 | async-start | bytes 4718592 | tf_op jit(solution)/shard_map/all_gather | solution.py:55
  7.9 372.2 %all-gather.15.cloned.1.call-start = ((), (), s32[]{:S(2)}) async-start(), calls=%async_computation.8 | async-start | bytes 4718592 | tf_op jit(solution)/shard_map/all_gather | solution.py:56
  8.7 549.7 %all-gather.13.cloned.1.call-start = ((), (), s32[]{:S(2)}) async-start(), calls=%async_computation.7 | async-start | bytes 4718592 | tf_op jit(solution)/shard_map/all_gather | solution.py:57
  9.4 614.1 %reduce-scatter.2.cloned.1.call-start = ((), (), s32[]{:S(2)}) async-start(), calls=%async_computation.4 | async-start | bytes 294912 | tf_op jit(solution)/shard_map/reduce_scatter | solution.py:60
  68.4 314.8 %copy-start.4 = (bf16[64,2048]{1,0:T(8,128)(2,1)}, bf16[64,2048]{1,0:T(8,128)(2,1)S(1)}, u32[]{:S(2)}) copy-start(bf16[64,2048]{1,0:T(8,128)(2,1)S(1)} %all_gather.23) | copy-start | bytes 786436
  153.8 404.6 %copy-start.5 = (bf16[64,2048]{1,0:T(8,128)(2,1)}, bf16[64,2048]{1,0:T(8,128)(2,1)S(1)}, u32[]{:S(2)}) copy-start(bf16[64,2048]{1,0:T(8,128)(2,1)S(1)} %all_gather.21) | copy-start | bytes 786436
  558.4 3.4 copy-start.2
  558.4 4.8 copy-start.3
  563.2 67.0 %copy-start.6 = (bf16[1,128,2048]{2,1,0:T(8,128)(2,1)S(1)}, bf16[1,128,2048]{2,1,0:T(8,128)(2,1)}, u32[]{:S(2)}) copy-start(bf16[1,128,2048]{2,1,0:T(8,128)(2,1)} %param.7) | copy-start | bytes 1572868
  565.4 173.6 %all-gather.9.cloned.1.call-start = ((), (), s32[]{:S(2)}) async-start(), calls=%async_computation.5 | async-start | bytes 2359296 | tf_op jit(solution)/shard_map/all_gather | solution.py:67
  565.9 288.4 %all-gather.11.cloned.1.call-start = ((), (), s32[]{:S(2)}) async-start(), calls=%async_computation.6 | async-start | bytes 2359296 | tf_op jit(solution)/shard_map/all_gather | solution.py:68
  567.2 19.1 %all-to-all-start = ((bf16[64,8,128]{2,0,1:T(8,128)(2,1)}), bf16[64,8,128]{2,0,1:T(8,128)(2,1)S(1)}, u32[]{:S(2)}, u32[]{:S(2)}) async-start(bf16[64,8,128]{2,0,1:T(8,128)(2,1)} %copy_bitcast_fusion.2), calls=%async_computation.1 | async-start | bytes 262144 | tf_op jit(solution)/shard_map/all_to_all | solution.py:62
  586.3 37.2 %all-to-all-start.1 = ((bf16[64,8,128]{2,0,1:T(8,128)(2,1)}), bf16[64,8,128]{2,0,1:T(8,128)(2,1)S(1)}, u32[]{:S(2)}, u32[]{:S(2)}) async-start(bf16[64,8,128]{2,0,1:T(8,128)(2,1)} %copy_bitcast_fusion.1), calls=%async_computation.2 | async-start | bytes 262144 | tf_op jit(solution)/shard_map/all_to_all | solution.py:63
  623.5 230.9 %all-to-all-start.2 = ((bf16[64,8,128]{2,0,1:T(8,128)(2,1)}), bf16[64,8,128]{2,0,1:T(8,128)(2,1)S(1)}, u32[]{:S(2)}, u32[]{:S(2)}) async-start(bf16[64,8,128]{2,0,1:T(8,128)(2,1)} %bitcast.74), calls=%async_computation.3 | async-start | bytes 262144 | tf_op jit(solution)/shard_map/all_to_all | solution.py:64
  631.3 226.2 %collective-permute-start = (bf16[128,2048]{1,0:T(8,128)(2,1)S(1)}, bf16[128,2048]{1,0:T(8,128)(2,1)S(1)}, u32[]{:S(2)}, u32[]{:S(2)}) collective-permute-start(bf16[128,2048]{1,0:T(8,128)(2,1)S(1)} %fusion.10), channel_id=1, source_target_pairs={{0,448},{64,0},{128,64},{192,128},{256,192},{320,256},{384,320},{4... | collective-permute-start | bytes 1572872 | tf_op jit(solution)/shard_map/ppermute | solution.py:12
  738.9 3.3 copy-start.1
Sparse Core Ops, SparseCore 0:
  11.1 191.3 all-gather.16
  205.5 174.5 all-gather.14
  383.2 175.0 all-gather.12
  565.5 57.9 reduce-scatter.1
  627.6 111.2 all-gather.8
  743.0 111.2 all-gather.10
where the time goes:
time: 866 us; the launch traced here: 865 us
  waiting for transfers between devices  663 us (77%)
  blocking collectives  141 us (16%)
  matrix products  23.4 us (3%)
  starting transfers between devices  18.5 us (2%)
  between operations  14.2 us (2%)
    all_gather x1, waiting for transfers between devices, body(): lax.all_gather(w_down[0], 'dp', axis=1, tiled=True)  175 us
    all_gather x1, waiting for transfers between devices, body(): lax.all_gather(w_up[0], 'dp', axis=1, tiled=True)  175 us
    all_gather x1, waiting for transfers between devices, body(): lax.all_gather(group_dy, 'dp', axis=0, tiled=True)  111 us
    all_gather x1, waiting for transfers between devices, body(): lax.all_gather(group_x, 'dp', axis=0, tiled=True)  108 us
    all_gather x1, blocking collectives, body(): lax.all_gather(send_dy, 'expert', axis=0, tiled=True)  84 us
    all_gather x1, blocking collectives, body(): lax.all_gather(send_x, 'expert', axis=0, tiled=True)  57.3 us
    all_gather x1, waiting for transfers between devices, body(): lax.all_gather(w_gate[0], 'dp', axis=1, tiled=True)  48.7 us
    reduce_scatter x1, waiting for transfers between devices, body(): lax.psum_scatter(d_part.astype(jnp.bfloat16), 'expert', scatter_dimension...  30.8 us
  transfers between devices with their start and end apart: 10, of which 7 were waited for; matrix products, arithmetic and copies ran while one was open for 2% of the time, Pallas kernels for 0%

commit v1 on v0

--- a/solution.py
+++ b/solution.py
@@ -64,7 +64,9 @@
         lax.all_to_all(hidden, "dp", split_axis=1, concat_axis=0, tiled=True),
     )
     every_x, every_dy = (
-        lax.all_gather(group_x, "dp", axis=0, tiled=True),
+        jnp.concatenate(
+            lax.all_to_all(jnp.stack([group_x] * lax.axis_size("dp")), "dp", 0, 0), axis=0
+        ),
         lax.all_gather(group_dy, "dp", axis=0, tiled=True),
     )
     part_gate, part_up, part_down = weight_grads(every_x, every_dy, own_gate, own_up, own_hidden)

time: 866 us -> 838 us (0.968)
  waiting for transfers between devices: 663 us -> 490 us
  blocking collectives: 141 us -> 266 us
  starting transfers between devices: 18.5 us -> 37.1 us
    all_gather x1, blocking collectives: 84 us -> 209 us  [body(): lax.all_gather(send_dy, 'expert', axis=0, tiled=True)]
    all_gather x1 -> x0, waiting for transfers between devices: 108 us -> none  [body(): lax.all_gather(group_x, 'dp', axis=0, tiled=True)]
    all_gather x1, waiting for transfers between devices: 48.7 us -> 0.01 us  [body(): lax.all_gather(w_gate[0], 'dp', axis=1, tiled=True)]
    all_to_all x0 -> x1, starting transfers between devices: none -> 17.2 us  [body(): lax.all_to_all(jnp.stack([group_x] * lax.axis_size('dp')), 'dp', 0, 0)]
    all_to_all x1, waiting for transfers between devices: 0.01 us -> 12.7 us  [body(): lax.all_to_all(d_up, 'dp', split_axis=1, concat_axis=0, tiled=True)]
    all_to_all x1, waiting for transfers between devices: 12.6 us -> 0.01 us  [body(): lax.all_to_all(d_gate, 'dp', split_axis=1, concat_axis=0, tiled=True)]
    all_gather x1, waiting for transfers between devices: 175 us -> 163 us  [body(): lax.all_gather(w_up[0], 'dp', axis=1, tiled=True)]
  transfers between devices with their start and end apart: 10 -> 10, of which waited for: 7 -> 5; matrix products, arithmetic and copies ran while one was open for 2% -> 3% of each run, Pallas kernels for 0% -> 0%
where the time goes in v1:
time: 838 us; the launch traced here: 837 us
  waiting for transfers between devices  490 us (58%)
  blocking collectives  266 us (32%)
  starting transfers between devices  37.1 us (4%)
  matrix products  23.1 us (3%)
  between operations  13.8 us (2%)
    all_gather x1, blocking collectives, body(): lax.all_gather(send_dy, 'expert', axis=0, tiled=True)  209 us
    all_gather x1, waiting for transfers between devices, body(): lax.all_gather(w_down[0], 'dp', axis=1, tiled=True)  174 us
    all_gather x1, waiting for transfers between devices, body(): lax.all_gather(w_up[0], 'dp', axis=1, tiled=True)  163 us
    all_gather x1, waiting for transfers between devices, body(): lax.all_gather(group_dy, 'dp', axis=0, tiled=True)  107 us
    all_gather x1, blocking collectives, body(): lax.all_gather(send_x, 'expert', axis=0, tiled=True)  57.2 us
    reduce_scatter x1, waiting for transfers between devices, body(): lax.psum_scatter(d_part.astype(jnp.bfloat16), 'expert', scatter_dimension...  30.5 us
    all_to_all x1, starting transfers between devices, body(): lax.all_to_all(jnp.stack([group_x] * lax.axis_size('dp')), 'dp', 0, 0)  17.2 us
  transfers between devices with their start and end apart: 10, of which 5 were waited for; matrix products, arithmetic and copies ran while one was open for 3% of the time, Pallas kernels for 0%

profile of v1, /device:TPU:16, one launch (start us, length us, event | category | flops | bytes accessed | tf_op | source)
XLA Modules:
  0.0 837.2 jit_solution(6762897580968210608)
XLA Ops:
  7.2 0.7 all-gather.14.cloned.1.call-update
  8.0 0.7 all-gather.12.cloned.1.call-update
  8.7 0.7 all-gather.10.cloned.1.call-update
  9.4 0.7 fusion.32
  10.2 0.7 fusion.31
  11.0 57.2 %all_gather.20 = bf16[64,2048]{1,0:T(8,128)(2,1)S(1)} all-gather(bf16[8,2048]{1,0:T(8,128)(2,1)S(1)} %convolution_convert_fusion.1), channel_id=1, replica_groups=mesh['section'=8,'expert'=8,'dp'=8] {'expert'}, dimensions={0}, use_global_device_ids=true | all-gather | bytes 294912 | tf_op jit(solution)/shard_map/all_gather | solution.py:51
  68.3 1.6 stack.2
  69.8 17.2 %all-to-all-start = ((bf16[8,64,2048]{2,1,0:T(8,128)(2,1)}), bf16[8,64,2048]{2,1,0:T(8,128)(2,1)S(1)}, u32[]{:S(2)}, u32[]{:S(2)}) async-start(bf16[8,64,2048]{2,1,0:T(8,128)(2,1)} %stack.2), calls=%async_computation.1 | async-start | bytes 4194304 | tf_op jit(solution)/shard_map/all_to_all | solution.py:68
  87.2 209.1 %all_gather.18 = bf16[64,2048]{1,0:T(8,128)(2,1)S(1)} all-gather(bf16[8,2048]{1,0:T(8,128)(2,1)S(1)} %convolution_convert_fusion.2), channel_id=1, replica_groups=mesh['section'=8,'expert'=8,'dp'=8] {'expert'}, dimensions={0}, use_global_device_ids=true | all-gather | bytes 294912 | tf_op jit(solution)/shard_map/all_gather | solution.py:52
  296.4 4.0 fusion.2
  300.4 162.6 %all-gather.12.cloned.1.call-done = bf16[1,2048,1024]{2,1,0:T(8,128)(2,1)} async-done(((bf16[1,2048,128]{2,1,0:T(8,128)(2,1)}), bf16[1,2048,1024]{2,1,0:T(8,128)(2,1)}) %all-gather.12.cloned.1.call-update) | async-done | bytes 4194320 | tf_op jit(solution)/shard_map/all_gather | solution.py:56
  463.0 3.7 fusion.6
  466.8 174.5 %all-gather.10.cloned.1.call-done = bf16[1,2048,1024]{2,1,0:T(8,128)(2,1)} async-done(((bf16[1,2048,128]{2,1,0:T(8,128)(2,1)}), bf16[1,2048,1024]{2,1,0:T(8,128)(2,1)}) %all-gather.10.cloned.1.call-update) | async-done | bytes 4194320 | tf_op jit(solution)/shard_map/all_gather | solution.py:57
  641.2 3.4 fusion.25
  644.8 1.4 fusion
  646.2 2.1 fusion.19
  648.4 0.5 all-gather.8.cloned.1.call-update
  649.0 0.7 copy_bitcast_fusion.1
  649.6 5.7 all-to-all-start.2
  655.4 0.7 copy.24
  656.1 12.7 %all-to-all-done.2 = bf16[64,8,128]{2,0,1:T(8,128)(2,1)S(1)} async-done(((bf16[64,8,128]{2,0,1:T(8,128)(2,1)}), bf16[64,8,128]{2,0,1:T(8,128)(2,1)S(1)}, u32[]{:S(2)}, u32[]{:S(2)}) %all-to-all-start.2) | async-done | bytes 131104 | tf_op jit(solution)/shard_map/all_to_all | solution.py:63
  668.8 0.7 copy-done.6
  669.4 5.9 all-to-all-start.3
  675.4 0.7 copy_bitcast_fusion.2
  676.0 30.5 %reduce-scatter.2.cloned.1.call-done = bf16[8,2048]{1,0:T(8,128)(2,1)} async-done(((bf16[64,2048]{1,0:T(8,128)(2,1)}), bf16[8,2048]{1,0:T(8,128)(2,1)}) %reduce-scatter.2.cloned.1.call-update) | async-done | bytes 32784 | tf_op jit(solution)/shard_map/reduce_scatter | solution.py:60
  706.5 1.9 fusion.12
  708.4 8.0 all-to-all-start.1
  716.4 107.1 %all-gather.8.cloned.1.call-done = bf16[512,2048]{1,0:T(8,128)(2,1)} async-done(((bf16[64,2048]{1,0:T(8,128)(2,1)}), bf16[512,2048]{1,0:T(8,128)(2,1)}) %all-gather.8.cloned.1.call-update) | async-done | bytes 2097168 | tf_op jit(solution)/shard_map/all_gather | solution.py:70
  823.6 3.1 fusion.16
  826.7 1.6 fusion.17
  828.3 1.6 fusion.18
  829.8 0.8 copy.26
  (30 shorter events, 0.9 us)
Async XLA Ops:
  7.2 3.7 copy-start
  7.2 289.2 %all-gather.14.cloned.1.call-start = ((), (), s32[]{:S(2)}) async-start(), calls=%async_computation.9 | async-start | bytes 4718592 | tf_op jit(solution)/shard_map/all_gather | solution.py:55
  7.9 79.1 %copy-start.4 = (bf16[1,128,2048]{2,1,0:T(8,128)(2,1)S(1)}, bf16[1,128,2048]{2,1,0:T(8,128)(2,1)}, u32[]{:S(2)}) copy-start(bf16[1,128,2048]{2,1,0:T(8,128)(2,1)} %param.7) | copy-start | bytes 1572868
  7.9 455.1 %all-gather.12.cloned.1.call-start = ((), (), s32[]{:S(2)}) async-start(), calls=%async_computation.8 | async-start | bytes 4718592 | tf_op jit(solution)/shard_map/all_gather | solution.py:56
  8.7 632.6 %all-gather.10.cloned.1.call-start = ((), (), s32[]{:S(2)}) async-start(), calls=%async_computation.7 | async-start | bytes 4718592 | tf_op jit(solution)/shard_map/all_gather | solution.py:57
  69.8 579.8 %all-to-all-start = ((bf16[8,64,2048]{2,1,0:T(8,128)(2,1)}), bf16[8,64,2048]{2,1,0:T(8,128)(2,1)S(1)}, u32[]{:S(2)}, u32[]{:S(2)}) async-start(bf16[8,64,2048]{2,1,0:T(8,128)(2,1)} %stack.2), calls=%async_computation.1 | async-start | bytes 4194304 | tf_op jit(solution)/shard_map/all_to_all | solution.py:68
  87.1 619.5 %reduce-scatter.2.cloned.1.call-start = ((), (), s32[]{:S(2)}) async-start(), calls=%async_computation.5 | async-start | bytes 294912 | tf_op jit(solution)/shard_map/reduce_scatter | solution.py:60
  296.4 344.9 %copy-start.3 = (bf16[64,2048]{1,0:T(8,128)(2,1)}, bf16[64,2048]{1,0:T(8,128)(2,1)S(1)}, u32[]{:S(2)}) copy-start(bf16[64,2048]{1,0:T(8,128)(2,1)S(1)} %all_gather.18) | copy-start | bytes 786436
  641.2 3.6 copy-start.1
  641.2 5.0 copy-start.2
  646.2 60.3 %copy-start.5 = (bf16[1,128,2048]{2,1,0:T(8,128)(2,1)S(1)}, bf16[1,128,2048]{2,1,0:T(8,128)(2,1)}, u32[]{:S(2)}) copy-start(bf16[1,128,2048]{2,1,0:T(8,128)(2,1)} %param.7) | copy-start | bytes 1572868
  648.4 175.2 %all-gather.8.cloned.1.call-start = ((), (), s32[]{:S(2)}) async-start(), calls=%async_computation.6 | async-start | bytes 2359296 | tf_op jit(solution)/shard_map/all_gather | solution.py:70
  649.6 19.1 %all-to-all-start.2 = ((bf16[64,8,128]{2,0,1:T(8,128)(2,1)}), bf16[64,8,128]{2,0,1:T(8,128)(2,1)S(1)}, u32[]{:S(2)}, u32[]{:S(2)}) async-start(bf16[64,8,128]{2,0,1:T(8,128)(2,1)} %copy_bitcast_fusion.1), calls=%async_computation.3 | async-start | bytes 262144 | tf_op jit(solution)/shard_map/all_to_all | solution.py:63
  668.8 0.7 copy-start.6
  669.4 39.0 %all-to-all-start.3 = ((bf16[64,8,128]{2,0,1:T(8,128)(2,1)}), bf16[64,8,128]{2,0,1:T(8,128)(2,1)S(1)}, u32[]{:S(2)}, u32[]{:S(2)}) async-start(bf16[64,8,128]{2,0,1:T(8,128)(2,1)} %bitcast.84), calls=%async_computation.4 | async-start | bytes 262144 | tf_op jit(solution)/shard_map/all_to_all | solution.py:64
  675.4 151.4 %copy-start.7 = (bf16[64,8,128]{2,0,1:T(8,128)(2,1)S(1)}, bf16[64,8,128]{2,0,1:T(8,128)(2,1)}, u32[]{:S(2)}) copy-start(bf16[64,8,128]{2,0,1:T(8,128)(2,1)} %copy-done.6) | copy-start | bytes 393220
  708.4 121.4 %collective-permute-start = (bf16[128,2048]{1,0:T(8,128)(2,1)}, bf16[128,2048]{1,0:T(8,128)(2,1)S(1)}, u32[]{:S(2)}, u32[]{:S(2)}) collective-permute-start(bf16[128,2048]{1,0:T(8,128)(2,1)} %fusion.12), channel_id=1, source_target_pairs={{0,448},{64,0},{128,64},{192,128},{256,192},{320,256},{384,320},{4... | collective-permute-start | bytes 1572872 | tf_op jit(solution)/shard_map/ppermute | solution.py:12
  708.4 119.9 %all-to-all-start.1 = ((bf16[64,8,128]{2,0,1:T(8,128)(2,1)}), bf16[64,8,128]{2,0,1:T(8,128)(2,1)S(1)}, u32[]{:S(2)}, u32[]{:S(2)}) async-start(bf16[64,8,128]{2,0,1:T(8,128)(2,1)} %copy_bitcast_fusion.2), calls=%async_computation.2 | async-start | bytes 262144 | tf_op jit(solution)/shard_map/all_to_all | solution.py:62
Sparse Core Ops, SparseCore 0:
  11.1 268.2 all-gather.13
  282.5 180.5 all-gather.11
  466.1 175.0 all-gather.9
  648.5 57.9 reduce-scatter.1
  710.6 112.8 all-gather.7
